TPU v7x, 256 devices: a whole 4x4x8 slice. The times are simulated.
256 devices in a mesh: grp: 16 (over x_hi, z), band: 16 (over y, x_lo, core).
Axes of the slice: x: 4 (x_hi: 2, x_lo: 2; x = x_hi * 2 + x_lo), y: 4, z: 8, core: 2. Of those that a mesh axis runs over, the one named last changes fastest.
Arguments:
- state: float32 [80, 384, 1280], P('grp', 'band'), may hold values from -6 to 6
- pair_of_slot: int32 [256], replicated, may hold values from 0 to 255, each once
- legendre: float32 [256, 513, 384], P(('grp', 'band')), may hold values from -0.3125 to 0.3125
- diffusion: float32 [80], replicated, may hold values from 0.5 to 8
- w_in: bfloat16 [80, 1024], replicated, may hold values from -0.625 to 0.625
- w_out: bfloat16 [1024, 80], replicated, may hold values from -0.1875 to 0.1875
Outputs:
- new_state: float32 [80, 384, 1280], P('grp', 'band')
Inputs may be any that keep to these rules, and one draw needn't show every extreme that they name: `pair_of_slot`: each pair index appears in exactly one slot.
All inputs are finite; a program needn't handle non-finite values.
Results may differ from a plain program's by a relative error of at most 0.004.
Values may be sent and summed in bfloat16 or wider, within the bound.
A program may use at most 64 MiB of HBM per device.

v0:
```python
import math

import jax
import jax.numpy as jnp
import numpy as np
from jax import lax
from jax.experimental import pallas as pl
from jax.experimental.pallas import tpu as pltpu
from jax.sharding import PartitionSpec as P

NLON = 1280
HALF = NLON // 2
M = 512
C5 = 5
LAT = 24
N = 16
ROWS = 528
TILES = 15
F32 = jnp.float32
BF16 = jnp.bfloat16


def transform_table():
    q = np.arange(128)
    lon = np.arange(HALF)
    blocks = []
    for parity in (0, 1):
        for j in range(4):
            p = 2 * q + (parity if j < 2 else 1 - parity)
            m = p if j < 2 else M - 1 - p
            phase = 2.0 * np.pi * ((m[:, None] * lon[None, :]) % NLON) / NLON
            blocks.append(np.cos(phase) if j % 2 == 0 else -np.sin(phase))
    return np.concatenate(blocks, 0).astype(jnp.bfloat16)


def kernel(
    state_h, pair_s, pair_v, leg_h, diff_s, win_h, wout_h, tab_h,
    out_ref,
    st, tab, leg, win, wout,
    s_send, s_recv, t_send, t_recv,
    f1_send, f1_recv, f2_send, f2_recv,
    b1_send, b1_recv, b2_send, b2_recv,
    mid, phys, xb, zf, fac, legb, legt, wint, woutt, ohf, oh, ohbg,
    load_sem, s_ss, s_rs, t_ss, t_rs, f1_ss, f1_rs, f2_ss, f2_rs, b1_ss, b1_rs, b2_ss, b2_rs,
):
    g = lax.axis_index("grp")
    b = lax.axis_index("band")

    loads = [
        pltpu.make_async_copy(src, dst, load_sem.at[i])
        for i, (src, dst) in enumerate(
            [(state_h, st), (tab_h, tab), (leg_h.at[0], leg), (win_h, win), (wout_h, wout)]
        )
    ]
    for load in loads:
        load.start()

    barrier = pltpu.get_barrier_semaphore()

    def greet(k, carry):
        pl.semaphore_signal(barrier, inc=1, device_id={"grp": lax.rem(g + k, N)}, device_id_type=pl.DeviceIdType.MESH)
        pl.semaphore_signal(barrier, inc=1, device_id={"band": lax.rem(b + k, N)}, device_id_type=pl.DeviceIdType.MESH)
        return carry

    lax.fori_loop(1, N, greet, 0)

    def exchange(axis, me, src, dst, ss, rs):
        def copy(k):
            other = lax.rem(me + k, N)
            return pltpu.make_async_remote_copy(
                src_ref=src.at[other], dst_ref=dst.at[me], send_sem=ss.at[other], recv_sem=rs.at[me],
                device_id={axis: other}, device_id_type=pl.DeviceIdType.MESH,
            )

        def arrival(k):
            other = lax.rem(me + k, N)
            return pltpu.make_async_remote_copy(
                src_ref=src.at[other], dst_ref=dst.at[other], send_sem=ss.at[other], recv_sem=rs.at[other],
                device_id={axis: other}, device_id_type=pl.DeviceIdType.MESH,
            )

        def start():
            lax.fori_loop(1, N, lambda k, c: (copy(k).start(), c)[1], 0)

        def recv():
            lax.fori_loop(1, N, lambda k, c: (arrival(k).wait_recv(), c)[1], 0)

        def sent():
            lax.fori_loop(1, N, lambda k, c: (copy(k).wait_send(), c)[1], 0)

        return start, recv, sent

    loads[0].wait()
    for a in range(3):
        for lp in range(5):
            block = st[:, 8 * a : 8 * a + 8, 256 * lp : 256 * lp + 256]
            stacked = jnp.concatenate([block[:, :, :128], block[:, :, 128:]], axis=1)
            s_send[a * 5 + lp] = stacked.reshape(80, 128).astype(BF16)

    pl.semaphore_wait(barrier, 2 * (N - 1))

    def s_copy(other):
        return pltpu.make_async_remote_copy(
            src_ref=s_send.at[other], dst_ref=s_recv.at[g], send_sem=s_ss.at[other], recv_sem=s_rs.at[g],
            device_id={"grp": other}, device_id_type=pl.DeviceIdType.MESH,
        )

    def s_start(k, carry):
        other = lax.rem(g + k, N)

        @pl.when(other < TILES)
        def _():
            s_copy(other).start()

        return carry

    lax.fori_loop(1, N, s_start, 0)

    rows = st[...].reshape(C5 * LAT, NLON)
    west, east = rows[:, :HALF], rows[:, HALF:]
    pad = jnp.zeros((8, HALF), F32)
    even = jnp.concatenate([west + east, pad], 0).astype(BF16)
    odd = jnp.concatenate([west - east, pad], 0).astype(BF16)
    value = 2 * (lax.broadcasted_iota(jnp.int32, (256, 256), 0) % 128) + lax.broadcasted_iota(jnp.int32, (256, 256), 0) // 128
    hot = (value == pair_v[...]).astype(F32)
    for h in range(2):
        ohf[256 * h : 256 * h + 256, :] = hot[128 * h : 128 * h + 128, :].T
        oh[:, 128 * h : 128 * h + 128] = ohf[256 * h : 256 * h + 256, :].astype(BF16)
        for k in range(N):
            turned = ohf[pl.ds(256 * h + k, N, stride=N), :].astype(BF16)
            ohbg[k * N : (k + 1) * N, 128 * h : 128 * h + 128] = turned
    loads[1].wait()
    nt = (((1,), (1,)), ((), ()))
    nn = (((1,), (0,)), ((), ()))
    ce = lax.dot_general(tab[:512, :], even, nt, preferred_element_type=F32).astype(BF16)
    co = lax.dot_general(tab[512:, :], odd, nt, preferred_element_type=F32).astype(BF16)
    for j in range(4):
        e, o = ce[128 * j : 128 * j + 128], co[128 * j : 128 * j + 128]
        natural = jnp.concatenate([e, o] if j < 2 else [o, e], 0)
        slots = lax.dot_general(ohbg[...], natural, nn, preferred_element_type=F32).astype(BF16)
        f1_send[:, 16 * j : 16 * j + 16, :] = slots.reshape(N, 16, 128)

    f1_start, f1_wait, f1_sent = exchange("band", b, f1_send, f1_recv, f1_ss, f1_rs)
    f1_start()
    f1_recv[b] = f1_send[b]

    p = pair_s[g * N + b]
    loads[2].wait()
    legb[0:512, :] = leg[0:512, :].astype(BF16)
    last = jnp.where(
        lax.broadcasted_iota(jnp.int32, (16, 384), 0) == 0, jnp.broadcast_to(leg[512:513, :], (16, 384)), 0.0
    )
    legb[512:528, :] = last.astype(BF16)
    legt[:, 0:512] = leg[0:512, :].T.astype(BF16)
    legt[:, 512:528] = last.T.astype(BF16)
    lane = lax.broadcasted_iota(jnp.int32, (1, 384), 1)
    chan = (lane % N) * C5 + jnp.minimum(2 * (lane // 128) + (lane % 128) // 64, C5 - 1)
    damping = jnp.zeros((1, 384), F32)
    for k in range(80):
        damping = jnp.where(chan == k, diff_s[k], damping)
    row = lax.broadcasted_iota(jnp.int32, (ROWS, 384), 0)
    first = row < M - p
    degree = jnp.where(first, p + row, row - 1).astype(F32)
    scaled = degree * (degree + 1.0) / F32(M * (M + 1))
    low = (lane % 64) < 32
    weight = jnp.where(low & (p == 0), F32(1.0 / NLON), F32(2.0 / NLON))
    fac[...] = jnp.where(first == low, jnp.exp(-damping * scaled) * weight, 0.0)
    loads[3].wait()
    loads[4].wait()
    wint[...] = win[...].astype(F32).T.astype(BF16)
    woutt[...] = wout[...].astype(F32).T.astype(BF16)

    def relay(src, dst):
        mid[...] = src[...].reshape(1024, 128).astype(F32)
        for k in range(N):
            for j in range(4):
                dst[k, 16 * j : 16 * j + 16, :] = mid[pl.ds(16 * j + k, N, stride=64), :].astype(BF16)

    f1_wait()
    relay(f1_recv, f2_send)
    f2_start, f2_wait, f2_sent = exchange("grp", g, f2_send, f2_recv, f2_ss, f2_rs)
    f2_start()
    f2_recv[g] = f2_send[g]

    def t_copy(other):
        return pltpu.make_async_remote_copy(
            src_ref=t_send.at[other], dst_ref=t_recv.at[g], send_sem=t_ss.at[other], recv_sem=t_rs.at[g],
            device_id={"grp": other}, device_id_type=pl.DeviceIdType.MESH,
        )

    @pl.when(g < TILES)
    def _():
        s_recv[g] = s_send[g]

        def arrive(k, carry):
            other = lax.rem(g + k, N)
            pltpu.make_async_remote_copy(
                src_ref=s_send.at[0], dst_ref=s_recv.at[other], send_sem=s_ss.at[0], recv_sem=s_rs.at[other],
                device_id={"grp": other}, device_id_type=pl.DeviceIdType.MESH,
            ).wait_recv()
            return carry

        lax.fori_loop(1, N, arrive, 0)
        phys[...] = s_recv[...].reshape(1280, 128).astype(F32)
        for i in range(16):
            xb[:, 128 * i : 128 * i + 128] = phys[pl.ds(i, 80, stride=16), :].astype(BF16)
        for i in range(8):
            x = xb[:, 256 * i : 256 * i + 256]
            half = lax.dot_general(wint[...], x, nn, preferred_element_type=F32) * 0.5
            hidden = (half + half * jnp.tanh(half)).astype(BF16)
            tend = lax.dot_general(woutt[...], hidden, nn, preferred_element_type=F32)
            phys[pl.ds(2 * i, 80, stride=16), :] = tend[:, :128]
            phys[pl.ds(2 * i + 1, 80, stride=16), :] = tend[:, 128:]
        t_send[...] = phys[...].reshape(N, 80, 128).astype(BF16)

        def send(k, carry):
            other = lax.rem(g + k, N)
            t_copy(other).start()
            return carry

        lax.fori_loop(1, N, send, 0)
        t_recv[g] = t_send[g]

    f2_wait()
    mid[...] = f2_recv[...].reshape(1024, 128).astype(F32)
    left = lax.broadcasted_iota(jnp.int32, (LAT, 128), 1) < 64
    for k in range(N):
        part = jnp.concatenate([mid[pl.ds(16 * j + k, N, stride=64), :] for j in range(4)], 0)
        turned = jnp.concatenate([part, part], 0).T
        at = slice(LAT * k, LAT * k + LAT)
        zf[at, 0:128] = jnp.where(left, turned[0:24], turned[24:48])
        zf[at, 128:256] = jnp.where(left, turned[48:72], turned[72:96])
        zf[at, 256:384] = turned[96:120]
    proj = lax.dot_general(legb[...], zf[...].astype(BF16), nn, preferred_element_type=F32)
    spec = (proj * fac[...]).astype(BF16)
    zf[...] = lax.dot_general(legt[...], spec, nn, preferred_element_type=F32)
    lanes = lax.broadcasted_iota(jnp.int32, (64, 128), 1)
    odd_chan = ((lanes // LAT) % 2) == 1
    for k in range(N):
        at = slice(LAT * k, LAT * k + LAT)
        t0, t1, t2 = zf[at, 0:128], zf[at, 128:256], zf[at, 256:384]
        turned = jnp.concatenate([t0, t0, t1, t1, t2, jnp.zeros((8, 128), F32)], 0).T
        b1_send[k] = jnp.where(odd_chan, turned[64:128], turned[0:64]).astype(BF16)

    b1_start, b1_wait, b1_sent = exchange("band", b, b1_send, b1_recv, b1_ss, b1_rs)
    b1_start()
    b1_recv[b] = b1_send[b]
    b1_wait()
    relay(b1_recv, b2_send)
    b2_start, b2_wait, b2_sent = exchange("grp", g, b2_send, b2_recv, b2_ss, b2_rs)
    b2_start()
    b2_recv[g] = b2_send[g]

    def t_arrive(k, carry):
        other = lax.rem(g + k, N)

        @pl.when(other < TILES)
        def _():
            pltpu.make_async_remote_copy(
                src_ref=t_send.at[0], dst_ref=t_recv.at[other], send_sem=t_ss.at[0], recv_sem=t_rs.at[other],
                device_id={"grp": other}, device_id_type=pl.DeviceIdType.MESH,
            ).wait_recv()

        return carry

    lax.fori_loop(1, N, t_arrive, 0)
    for a in range(3):
        for lp in range(5):
            block = t_recv[a * 5 + lp].astype(F32).reshape(C5, 16, 128)
            out_ref[:, 8 * a : 8 * a + 8, 256 * lp : 256 * lp + 128] = block[:, 0:8]
            out_ref[:, 8 * a : 8 * a + 8, 256 * lp + 128 : 256 * lp + 256] = block[:, 8:16]

    b2_wait()
    natural = []
    for j in range(4):
        slots = b2_recv[:, 16 * j : 16 * j + 16, :].reshape(256, 128).astype(F32).T.astype(BF16)
        natural.append(lax.dot_general(slots, oh[...], nn, preferred_element_type=F32).astype(BF16))
    n0, n1, n2, n3 = natural
    even = jnp.concatenate([n0[:, :128], n1[:, :128], n2[:, 128:], n3[:, 128:]], 1)
    odd = jnp.concatenate([n0[:, 128:], n1[:, 128:], n2[:, :128], n3[:, :128]], 1)
    even = lax.dot_general(even, tab[:512, :], nn, preferred_element_type=F32)
    odd = lax.dot_general(odd, tab[512:, :], nn, preferred_element_type=F32)
    west = (even + odd)[:120].reshape(C5, LAT, HALF)
    east = (even - odd)[:120].reshape(C5, LAT, HALF)
    out_ref[:, :, :HALF] += west
    out_ref[:, :, HALF:] += east

    def s_sent(k, carry):
        other = lax.rem(g + k, N)

        @pl.when(other < TILES)
        def _():
            s_copy(other).wait_send()

        return carry

    lax.fori_loop(1, N, s_sent, 0)

    @pl.when(g < TILES)
    def _():
        lax.fori_loop(1, N, lambda k, c: (t_copy(lax.rem(g + k, N)).wait_send(), c)[1], 0)

    f1_sent()
    f2_sent()
    b1_sent()
    b2_sent()


def shards(state, pair_of_slot, legendre, diffusion, w_in, w_out):
    table = jnp.asarray(transform_table())
    hbm = pl.BlockSpec(memory_space=pl.ANY)
    smem = pl.BlockSpec(memory_space=pltpu.SMEM)
    vmem = pl.BlockSpec(memory_space=pltpu.VMEM)
    dma = pltpu.SemaphoreType.DMA
    message = pltpu.VMEM((N, 64, 128), BF16)
    block = pltpu.VMEM((N, 80, 128), BF16)
    return pl.pallas_call(
        kernel,
        out_shape=jax.ShapeDtypeStruct(state.shape, F32),
        in_specs=[hbm, smem, vmem, hbm, smem, hbm, hbm, hbm],
        out_specs=vmem,
        scratch_shapes=[
            pltpu.VMEM(state.shape, F32),
            pltpu.VMEM((1024, HALF), BF16),
            pltpu.VMEM((513, 384), F32),
            pltpu.VMEM((80, 1024), BF16),
            pltpu.VMEM((1024, 80), BF16),
            *[block] * 4,
            *[message] * 8,
            pltpu.VMEM((1024, 128), F32),
            pltpu.VMEM((1280, 128), F32),
            pltpu.VMEM((80, 2048), BF16),
            pltpu.VMEM((384, 384), F32),
            pltpu.VMEM((ROWS, 384), F32),
            pltpu.VMEM((ROWS, 384), BF16),
            pltpu.VMEM((384, ROWS), BF16),
            pltpu.VMEM((1024, 80), BF16),
            pltpu.VMEM((80, 1024), BF16),
            pltpu.VMEM((512, 128), F32),
            pltpu.VMEM((256, 256), BF16),
            pltpu.VMEM((256, 256), BF16),
            dma((5,)),
            *[dma((N,))] * 12,
        ],
        compiler_params=pltpu.CompilerParams(
            collective_id=0, has_side_effects=True, vmem_limit_bytes=40 * 1024 * 1024
        ),
        cost_estimate=pl.CostEstimate(flops=2_500_000_000, bytes_accessed=4_000_000, transcendentals=2_400_000),
    )(state, pair_of_slot, pair_of_slot.reshape(1, 256), legendre, diffusion, w_in, w_out, table)


def solution(mesh):
    return jax.shard_map(
        shards,
        mesh=mesh,
        in_specs=(P("grp", "band", None), P(), P(("grp", "band"), None, None), P(), P(), P()),
        out_specs=P("grp", "band", None),
        check_vma=False,
    )
```

profile of v0, /device:TPU:1, one launch (start us, length us, event | category | flops | bytes accessed | tf_op | source)
XLA Modules:
  0.0 55.2 jit_solution(9791299974410997705)
XLA Ops:
  0.0 0.0 copy-start.2
  0.0 0.0 copy-start.1
  0.0 0.0 copy-start.3
  0.0 0.0 copy-start
  0.0 1.2 %copy.9.wout_h = bf16[1024,80]{1,0:T(8,128)(2,1)S(1)} copy(bf16[1024,80]{0,1:T(8,128)(2,1)} %param.12) | data formatting | bytes 327680 | tf_op args[5]
  1.2 1.2 %copy.8.leg_h = f32[1,513,384]{2,1,0:T(8,128)S(1)} copy(f32[1,513,384]{2,0,1:T(1,128)} %param.9) | data formatting | bytes 1575936 | tf_op args[2]
  2.4 0.0 copy-done.2
  2.4 0.0 copy-done.1
  2.4 0.0 copy-done.3
  2.4 0.0 copy-done
  2.4 0.0 copy-start.4
  2.4 1.3 %copy-done.4 = bf16[1024,640]{1,0:T(8,128)(2,1)S(1)} copy-done((bf16[1024,640]{1,0:T(8,128)(2,1)S(1)}, bf16[1024,640]{1,0:T(8,128)(2,1)}, u32[]{:S(2)}) %copy-start.4) | copy-done | bytes 1310744
  3.7 50.6 %shard_map.73 = f32[5,24,1280]{2,1,0:T(8,128)S(1)} custom-call(f32[5,24,1280]{2,1,0:T(8,128)S(1)} %copy-done, s32[256]{0:T(256)S(1)} %copy-done.2, s32[1,256]{1,0:T(1,128)S(1)} %bitcast.1, f32[1,513,384]{2,1,0:T(8,128)S(1)} %copy.8.leg_h, f32[80]{0:T(128)S(1)} %copy-done.3, bf16[80,1024]{1,0:T(8,128)(2,1)S(1)} %copy-done.1, ...), custom_call_target="tpu_custom_call" | custom-call | flops 2500000000 | bytes 4000000 | tf_op jit(solution)/shard_map/pallas_call | solution.py:317
  54.4 0.8 %copy.11 = f32[5,24,1280]{2,1,0:T(8,128)} copy(f32[5,24,1280]{2,1,0:T(8,128)S(1)} %shard_map.73) | data formatting | bytes 1228800
Async XLA Ops:
  0.0 2.4 %copy-start.2 = (s32[256]{0:T(256)S(1)}, s32[256]{0:T(256)}, u32[]{:S(2)}) copy-start(s32[256]{0:T(256)} %pair_s.1) | copy-start | bytes 3076
  0.0 2.4 %copy-start.1 = (bf16[80,1024]{1,0:T(8,128)(2,1)S(1)}, bf16[80,1024]{1,0:T(8,128)(2,1)}, u32[]{:S(2)}) copy-start(bf16[80,1024]{1,0:T(8,128)(2,1)} %win_h.1) | copy-start | bytes 491524
  0.0 2.4 %copy-start.3 = (f32[80]{0:T(128)S(1)}, f32[80]{0:T(128)}, u32[]{:S(2)}) copy-start(f32[80]{0:T(128)} %diff_s.1) | copy-start | bytes 964
  0.0 2.4 %copy-start = (f32[5,24,1280]{2,1,0:T(8,128)S(1)}, f32[5,24,1280]{2,1,0:T(8,128)}, u32[]{:S(2)}) copy-start(f32[5,24,1280]{2,1,0:T(8,128)} %state_h.1) | copy-start | bytes 1843204
  2.4 1.3 %copy-start.4 = (bf16[1024,640]{1,0:T(8,128)(2,1)S(1)}, bf16[1024,640]{1,0:T(8,128)(2,1)}, u32[]{:S(2)}) copy-start(bf16[1024,640]{1,0:T(8,128)(2,1)} %constant.2.clone.tab_h) | copy-start | bytes 3932164
where the time goes:
time: 55.6 us; the launch traced here: 55.2 us
  Pallas kernels  50.6 us (91%)
  local copies, waits for them, and re-layouts  4.5 us (8%)
    pallas_call x1, Pallas kernels, shards(): pl.pallas_call(kernel, out_shape=jax.ShapeDtypeStruct(state.shape, F32),...  50.6 us
    unnamed x13, local copies, waits for them, and re-layouts  4.5 us

commit v1 on v0

--- a/solution.py
+++ b/solution.py
@@ -34,13 +34,13 @@
 
 
 def kernel(
-    state_h, pair_s, pair_v, leg_h, diff_s, win_h, wout_h, tab_h,
+    state_h, pair_s, pair_v, leg_h, diff_s, win_h, woutt_h, tab_h,
     out_ref,
-    st, tab, leg, win, wout,
+    st, tab, leg, win, woutt,
     s_send, s_recv, t_send, t_recv,
     f1_send, f1_recv, f2_send, f2_recv,
     b1_send, b1_recv, b2_send, b2_recv,
-    mid, phys, xb, zf, fac, legb, legt, wint, woutt, ohf, oh, ohbg,
+    mid, phys, xb, zf, fac, legb, legt, wint, ohf, oh, ohbg,
     load_sem, s_ss, s_rs, t_ss, t_rs, f1_ss, f1_rs, f2_ss, f2_rs, b1_ss, b1_rs, b2_ss, b2_rs,
 ):
     g = lax.axis_index("grp")
@@ -49,7 +49,7 @@
     loads = [
         pltpu.make_async_copy(src, dst, load_sem.at[i])
         for i, (src, dst) in enumerate(
-            [(state_h, st), (tab_h, tab), (leg_h.at[0], leg), (win_h, win), (wout_h, wout)]
+            [(state_h, st), (tab_h, tab), (leg_h, leg), (win_h, win), (woutt_h, woutt)]
         )
     ]
     for load in loads:
@@ -64,31 +64,36 @@
 
     lax.fori_loop(1, N, greet, 0)
 
-    def exchange(axis, me, src, dst, ss, rs):
-        def copy(k):
-            other = lax.rem(me + k, N)
-            return pltpu.make_async_remote_copy(
-                src_ref=src.at[other], dst_ref=dst.at[me], send_sem=ss.at[other], recv_sem=rs.at[me],
-                device_id={axis: other}, device_id_type=pl.DeviceIdType.MESH,
-            )
-
-        def arrival(k):
-            other = lax.rem(me + k, N)
-            return pltpu.make_async_remote_copy(
-                src_ref=src.at[other], dst_ref=dst.at[other], send_sem=ss.at[other], recv_sem=rs.at[other],
-                device_id={axis: other}, device_id_type=pl.DeviceIdType.MESH,
-            )
-
+    def targets(axis):
+        if axis == "grp":
+            steps = sorted(((x, z) for x in range(2) for z in range(8)), key=lambda s: -(2 * s[0] + min(s[1], 8 - s[1])))
+            return [lax.rem(g // 8 + x, 2) * 8 + lax.rem(g % 8 + z, 8) for x, z in steps[:-1]]
+        steps = sorted(
+            ((y, x, c) for y in range(4) for x in range(2) for c in range(2)),
+            key=lambda s: -(2 * min(s[0], 4 - s[0]) + 2 * s[1] + s[2]),
+        )
+        return [
+            lax.rem(b // 4 + y, 4) * 4 + lax.rem(b // 2 % 2 + x, 2) * 2 + lax.rem(b % 2 + c, 2) for y, x, c in steps[:-1]
+        ]
+
+    def message(axis, src, dst, ss, rs, other):
+        return pltpu.make_async_remote_copy(
+            src_ref=src.at[other], dst_ref=dst.at[{"grp": g, "band": b}[axis]], send_sem=ss, recv_sem=rs,
+            device_id={axis: other}, device_id_type=pl.DeviceIdType.MESH,
+        )
+
+    def bulk(axis, src, dst, ss, rs, count):
+        return pltpu.make_async_remote_copy(
+            src_ref=src.at[pl.ds(0, count)], dst_ref=dst.at[pl.ds(0, count)], send_sem=ss, recv_sem=rs,
+            device_id={axis: lax.rem({"grp": g, "band": b}[axis] + 1, N)}, device_id_type=pl.DeviceIdType.MESH,
+        )
+
+    def exchange(*refs):
         def start():
-            lax.fori_loop(1, N, lambda k, c: (copy(k).start(), c)[1], 0)
-
-        def recv():
-            lax.fori_loop(1, N, lambda k, c: (arrival(k).wait_recv(), c)[1], 0)
-
-        def sent():
-            lax.fori_loop(1, N, lambda k, c: (copy(k).wait_send(), c)[1], 0)
-
-        return start, recv, sent
+            for other in targets(refs[0]):
+                message(*refs, other).start()
+
+        return start, bulk(*refs, N - 1).wait_recv, bulk(*refs, N - 1).wait_send
 
     loads[0].wait()
     for a in range(3):
@@ -96,25 +101,6 @@
             block = st[:, 8 * a : 8 * a + 8, 256 * lp : 256 * lp + 256]
             stacked = jnp.concatenate([block[:, :, :128], block[:, :, 128:]], axis=1)
             s_send[a * 5 + lp] = stacked.reshape(80, 128).astype(BF16)
-
-    pl.semaphore_wait(barrier, 2 * (N - 1))
-
-    def s_copy(other):
-        return pltpu.make_async_remote_copy(
-            src_ref=s_send.at[other], dst_ref=s_recv.at[g], send_sem=s_ss.at[other], recv_sem=s_rs.at[g],
-            device_id={"grp": other}, device_id_type=pl.DeviceIdType.MESH,
-        )
-
-    def s_start(k, carry):
-        other = lax.rem(g + k, N)
-
-        @pl.when(other < TILES)
-        def _():
-            s_copy(other).start()
-
-        return carry
-
-    lax.fori_loop(1, N, s_start, 0)
 
     rows = st[...].reshape(C5 * LAT, NLON)
     west, east = rows[:, :HALF], rows[:, HALF:]
@@ -140,18 +126,26 @@
         slots = lax.dot_general(ohbg[...], natural, nn, preferred_element_type=F32).astype(BF16)
         f1_send[:, 16 * j : 16 * j + 16, :] = slots.reshape(N, 16, 128)
 
-    f1_start, f1_wait, f1_sent = exchange("band", b, f1_send, f1_recv, f1_ss, f1_rs)
+    f1_start, f1_wait, f1_sent = exchange("band", f1_send, f1_recv, f1_ss, f1_rs)
+    pl.semaphore_wait(barrier, 2 * (N - 1))
     f1_start()
+    states = ("grp", s_send, s_recv, s_ss, s_rs)
+    for other in targets("grp"):
+
+        @pl.when(other < TILES)
+        def _(other=other):
+            message(*states, other).start()
+
     f1_recv[b] = f1_send[b]
 
     p = pair_s[g * N + b]
     loads[2].wait()
-    legb[0:512, :] = leg[0:512, :].astype(BF16)
+    legb[0:512, :] = leg[0:512].reshape(512, 384).astype(BF16)
     last = jnp.where(
-        lax.broadcasted_iota(jnp.int32, (16, 384), 0) == 0, jnp.broadcast_to(leg[512:513, :], (16, 384)), 0.0
+        lax.broadcasted_iota(jnp.int32, (16, 384), 0) == 0, jnp.broadcast_to(leg[512], (16, 384)), 0.0
     )
     legb[512:528, :] = last.astype(BF16)
-    legt[:, 0:512] = leg[0:512, :].T.astype(BF16)
+    legt[:, 0:512] = leg[0:512].reshape(512, 384).T.astype(BF16)
     legt[:, 512:528] = last.T.astype(BF16)
     lane = lax.broadcasted_iota(jnp.int32, (1, 384), 1)
     chan = (lane % N) * C5 + jnp.minimum(2 * (lane // 128) + (lane % 128) // 64, C5 - 1)
@@ -168,7 +162,6 @@
     loads[3].wait()
     loads[4].wait()
     wint[...] = win[...].astype(F32).T.astype(BF16)
-    woutt[...] = wout[...].astype(F32).T.astype(BF16)
 
     def relay(src, dst):
         mid[...] = src[...].reshape(1024, 128).astype(F32)
@@ -178,29 +171,16 @@
 
     f1_wait()
     relay(f1_recv, f2_send)
-    f2_start, f2_wait, f2_sent = exchange("grp", g, f2_send, f2_recv, f2_ss, f2_rs)
+    f2_start, f2_wait, f2_sent = exchange("grp", f2_send, f2_recv, f2_ss, f2_rs)
     f2_start()
     f2_recv[g] = f2_send[g]
 
-    def t_copy(other):
-        return pltpu.make_async_remote_copy(
-            src_ref=t_send.at[other], dst_ref=t_recv.at[g], send_sem=t_ss.at[other], recv_sem=t_rs.at[g],
-            device_id={"grp": other}, device_id_type=pl.DeviceIdType.MESH,
-        )
+    tendencies = ("grp", t_send, t_recv, t_ss, t_rs)
 
     @pl.when(g < TILES)
     def _():
         s_recv[g] = s_send[g]
-
-        def arrive(k, carry):
-            other = lax.rem(g + k, N)
-            pltpu.make_async_remote_copy(
-                src_ref=s_send.at[0], dst_ref=s_recv.at[other], send_sem=s_ss.at[0], recv_sem=s_rs.at[other],
-                device_id={"grp": other}, device_id_type=pl.DeviceIdType.MESH,
-            ).wait_recv()
-            return carry
-
-        lax.fori_loop(1, N, arrive, 0)
+        bulk(*states, N - 1).wait_recv()
         phys[...] = s_recv[...].reshape(1280, 128).astype(F32)
         for i in range(16):
             xb[:, 128 * i : 128 * i + 128] = phys[pl.ds(i, 80, stride=16), :].astype(BF16)
@@ -213,13 +193,19 @@
             phys[pl.ds(2 * i + 1, 80, stride=16), :] = tend[:, 128:]
         t_send[...] = phys[...].reshape(N, 80, 128).astype(BF16)
 
-        def send(k, carry):
-            other = lax.rem(g + k, N)
-            t_copy(other).start()
-            return carry
-
-        lax.fori_loop(1, N, send, 0)
+        for other in targets("grp"):
+            message(*tendencies, other).start()
         t_recv[g] = t_send[g]
+
+    f1_sent()
+
+    @pl.when(g < TILES)
+    def _():
+        bulk(*states, TILES - 1).wait_send()
+
+    @pl.when(g >= TILES)
+    def _():
+        bulk(*states, TILES).wait_send()
 
     f2_wait()
     mid[...] = f2_recv[...].reshape(1024, 128).astype(F32)
@@ -242,34 +228,32 @@
         turned = jnp.concatenate([t0, t0, t1, t1, t2, jnp.zeros((8, 128), F32)], 0).T
         b1_send[k] = jnp.where(odd_chan, turned[64:128], turned[0:64]).astype(BF16)
 
-    b1_start, b1_wait, b1_sent = exchange("band", b, b1_send, b1_recv, b1_ss, b1_rs)
+    b1_start, b1_wait, b1_sent = exchange("band", b1_send, b1_recv, b1_ss, b1_rs)
     b1_start()
     b1_recv[b] = b1_send[b]
+    f2_sent()
     b1_wait()
     relay(b1_recv, b2_send)
-    b2_start, b2_wait, b2_sent = exchange("grp", g, b2_send, b2_recv, b2_ss, b2_rs)
+    b2_start, b2_wait, b2_sent = exchange("grp", b2_send, b2_recv, b2_ss, b2_rs)
     b2_start()
     b2_recv[g] = b2_send[g]
 
-    def t_arrive(k, carry):
-        other = lax.rem(g + k, N)
-
-        @pl.when(other < TILES)
-        def _():
-            pltpu.make_async_remote_copy(
-                src_ref=t_send.at[0], dst_ref=t_recv.at[other], send_sem=t_ss.at[0], recv_sem=t_rs.at[other],
-                device_id={"grp": other}, device_id_type=pl.DeviceIdType.MESH,
-            ).wait_recv()
-
-        return carry
-
-    lax.fori_loop(1, N, t_arrive, 0)
+    @pl.when(g < TILES)
+    def _():
+        bulk(*tendencies, TILES - 1).wait_recv()
+        bulk(*tendencies, N - 1).wait_send()
+
+    @pl.when(g >= TILES)
+    def _():
+        bulk(*tendencies, TILES).wait_recv()
+
     for a in range(3):
         for lp in range(5):
             block = t_recv[a * 5 + lp].astype(F32).reshape(C5, 16, 128)
             out_ref[:, 8 * a : 8 * a + 8, 256 * lp : 256 * lp + 128] = block[:, 0:8]
             out_ref[:, 8 * a : 8 * a + 8, 256 * lp + 128 : 256 * lp + 256] = block[:, 8:16]
 
+    b1_sent()
     b2_wait()
     natural = []
     for j in range(4):
@@ -285,30 +269,12 @@
     out_ref[:, :, :HALF] += west
     out_ref[:, :, HALF:] += east
 
-    def s_sent(k, carry):
-        other = lax.rem(g + k, N)
-
-        @pl.when(other < TILES)
-        def _():
-            s_copy(other).wait_send()
-
-        return carry
-
-    lax.fori_loop(1, N, s_sent, 0)
-
-    @pl.when(g < TILES)
-    def _():
-        lax.fori_loop(1, N, lambda k, c: (t_copy(lax.rem(g + k, N)).wait_send(), c)[1], 0)
-
-    f1_sent()
-    f2_sent()
-    b1_sent()
     b2_sent()
 
 
 def shards(state, pair_of_slot, legendre, diffusion, w_in, w_out):
     table = jnp.asarray(transform_table())
-    hbm = pl.BlockSpec(memory_space=pl.ANY)
+    hbm = pl.BlockSpec(memory_space=pltpu.HBM)
     smem = pl.BlockSpec(memory_space=pltpu.SMEM)
     vmem = pl.BlockSpec(memory_space=pltpu.VMEM)
     dma = pltpu.SemaphoreType.DMA
@@ -322,9 +288,9 @@
         scratch_shapes=[
             pltpu.VMEM(state.shape, F32),
             pltpu.VMEM((1024, HALF), BF16),
-            pltpu.VMEM((513, 384), F32),
+            pltpu.VMEM((513, 1, 384), F32),
             pltpu.VMEM((80, 1024), BF16),
-            pltpu.VMEM((1024, 80), BF16),
+            pltpu.VMEM((80, 1024), BF16),
             *[block] * 4,
             *[message] * 8,
             pltpu.VMEM((1024, 128), F32),
@@ -335,18 +301,17 @@
             pltpu.VMEM((ROWS, 384), BF16),
             pltpu.VMEM((384, ROWS), BF16),
             pltpu.VMEM((1024, 80), BF16),
-            pltpu.VMEM((80, 1024), BF16),
             pltpu.VMEM((512, 128), F32),
             pltpu.VMEM((256, 256), BF16),
             pltpu.VMEM((256, 256), BF16),
             dma((5,)),
-            *[dma((N,))] * 12,
+            *[dma] * 12,
         ],
         compiler_params=pltpu.CompilerParams(
-            collective_id=0, has_side_effects=True, vmem_limit_bytes=40 * 1024 * 1024
+            collective_id=0, has_side_effects=True, vmem_limit_bytes=56 * 1024 * 1024
         ),
         cost_estimate=pl.CostEstimate(flops=2_500_000_000, bytes_accessed=4_000_000, transcendentals=2_400_000),
-    )(state, pair_of_slot, pair_of_slot.reshape(1, 256), legendre, diffusion, w_in, w_out, table)
+    )(state, pair_of_slot, pair_of_slot.reshape(1, 256), jnp.swapaxes(legendre, 0, 1), diffusion, w_in, w_out.T, table)
 
 
 def solution(mesh):

time: 55.6 us -> 47 us (0.85)
  Pallas kernels: 50.6 us -> 44.9 us
  local copies, waits for them, and re-layouts: 4.5 us -> 1.94 us
    pallas_call x1, Pallas kernels: 50.6 us -> 44.9 us  [shards(): pl.pallas_call(kernel, out_shape=jax.ShapeDtypeStruct(state.shape, F32),...]
    unnamed x13 -> x1, local copies, waits for them, and re-layouts: 4.5 us -> 1.94 us
where the time goes in v1:
time: 47 us; the launch traced here: 46.8 us
  Pallas kernels  44.9 us (96%)
  local copies, waits for them, and re-layouts  1.94 us (4%)
    pallas_call x1, Pallas kernels, shards(): pl.pallas_call(kernel, out_shape=jax.ShapeDtypeStruct(state.shape, F32),...  44.9 us
    unnamed x1, local copies, waits for them, and re-layouts  1.94 us

profile of v1, /device:TPU:1, one launch (start us, length us, event | category | flops | bytes accessed | tf_op | source)
XLA Modules:
  0.0 46.8 jit_solution(7231689084767445195)
XLA Ops:
  0.0 44.9 %shard_map.73 = f32[5,24,1280]{2,1,0:T(8,128)} custom-call(f32[5,24,1280]{2,1,0:T(8,128)} %state_h.1, s32[256]{0:T(256)} %pair_s.1, s32[1,256]{1,0:T(1,128)} %bitcast.5, f32[513,1,384]{2,1,0:T(1,128)} %bitcast.3, f32[80]{0:T(128)} %diff_s.1, bf16[80,1024]{1,0:T(8,128)(2,1)} %win_h.1, bf16[80,1024]{1,0:T(8,128)(2,1)} %bitcast.4, ...), custom_call_target="tpu_custom_call" | custom-call | flops 2500000000 | bytes 4000000 | tf_op jit(solution)/shard_map/pallas_call | solution.py:283
  44.9 1.9 %copy.9 = f32[5,24,1280]{2,1,0:T(8,128)} copy(f32[5,24,1280]{2,1,0:T(8,128)} %shard_map.73) | data formatting | bytes 1228800

commit v2 on v1

--- a/solution.py
+++ b/solution.py
@@ -15,6 +15,7 @@
 LAT = 24
 N = 16
 ROWS = 528
+EARLY = 4
 TILES = 15
 F32 = jnp.float32
 BF16 = jnp.bfloat16
@@ -34,14 +35,16 @@
 
 
 def kernel(
-    state_h, pair_s, pair_v, leg_h, diff_s, win_h, woutt_h, tab_h,
+    state_h, pair_h, pairv_h, leg_h, diff_h, win_h, woutt_h, tab_h,
     out_ref,
-    st, tab, leg, win, woutt,
+    st, tab, leg, win, woutt, pair_s, pair_v, diff_s,
     s_send, s_recv, t_send, t_recv,
-    f1_send, f1_recv, f2_send, f2_recv,
-    b1_send, b1_recv, b2_send, b2_recv,
-    mid, phys, xb, zf, fac, legb, legt, wint, ohf, oh, ohbg,
-    load_sem, s_ss, s_rs, t_ss, t_rs, f1_ss, f1_rs, f2_ss, f2_rs, b1_ss, b1_rs, b2_ss, b2_rs,
+    f1_send, f1_recv, f2_send, f2_recv, h1_send, h1_recv, h2_send, h2_recv,
+    b1_send, b1_recv, b2_send, b2_recv, c1_send, c1_recv, c2_send, c2_recv,
+    mid, mid2, phys, xb, zf, fac, legb, legt, wint, ohf, oh, ohbg,
+    load_sem, s_ss, s_rs, t_ss, t_rs,
+    f1_ss, f1_rs, f2_ss, f2_rs, h1_ss, h1_rs, h2_ss, h2_rs,
+    b1_ss, b1_rs, b2_ss, b2_rs, c1_ss, c1_rs, c2_ss, c2_rs,
 ):
     g = lax.axis_index("grp")
     b = lax.axis_index("band")
@@ -49,7 +52,8 @@
     loads = [
         pltpu.make_async_copy(src, dst, load_sem.at[i])
         for i, (src, dst) in enumerate(
-            [(state_h, st), (tab_h, tab), (leg_h, leg), (win_h, win), (woutt_h, woutt)]
+            [(state_h, st), (tab_h, tab), (leg_h, leg), (win_h, win), (woutt_h, woutt),
+             (pair_h, pair_s), (pairv_h, pair_v), (diff_h, diff_s)]
         )
     ]
     for load in loads:
@@ -108,6 +112,7 @@
     even = jnp.concatenate([west + east, pad], 0).astype(BF16)
     odd = jnp.concatenate([west - east, pad], 0).astype(BF16)
     value = 2 * (lax.broadcasted_iota(jnp.int32, (256, 256), 0) % 128) + lax.broadcasted_iota(jnp.int32, (256, 256), 0) // 128
+    loads[6].wait()
     hot = (value == pair_v[...]).astype(F32)
     for h in range(2):
         ohf[256 * h : 256 * h + 256, :] = hot[128 * h : 128 * h + 128, :].T
@@ -123,11 +128,16 @@
     for j in range(4):
         e, o = ce[128 * j : 128 * j + 128], co[128 * j : 128 * j + 128]
         natural = jnp.concatenate([e, o] if j < 2 else [o, e], 0)
-        slots = lax.dot_general(ohbg[...], natural, nn, preferred_element_type=F32).astype(BF16)
-        f1_send[:, 16 * j : 16 * j + 16, :] = slots.reshape(N, 16, 128)
+        order, dst = (ohbg, f1_send) if j < 2 else (oh, h1_send)
+        slots = lax.dot_general(order[...], natural, nn, preferred_element_type=F32).astype(BF16)
+        dst[:, 16 * (j % 2) : 16 * (j % 2) + 16, :] = slots.reshape(N, 16, 128)
 
     f1_start, f1_wait, f1_sent = exchange("band", f1_send, f1_recv, f1_ss, f1_rs)
+    f2_start, f2_wait, f2_sent = exchange("grp", f2_send, f2_recv, f2_ss, f2_rs)
+    h1_start, h1_wait, h1_sent = exchange("grp", h1_send, h1_recv, h1_ss, h1_rs)
+    h2_start, h2_wait, h2_sent = exchange("band", h2_send, h2_recv, h2_ss, h2_rs)
     pl.semaphore_wait(barrier, 2 * (N - 1))
+    h1_start()
     f1_start()
     states = ("grp", s_send, s_recv, s_ss, s_rs)
     for other in targets("grp"):
@@ -137,7 +147,10 @@
             message(*states, other).start()
 
     f1_recv[b] = f1_send[b]
-
+    h1_recv[g] = h1_send[g]
+
+    loads[5].wait()
+    loads[7].wait()
     p = pair_s[g * N + b]
     loads[2].wait()
     legb[0:512, :] = leg[0:512].reshape(512, 384).astype(BF16)
@@ -161,21 +174,32 @@
     fac[...] = jnp.where(first == low, jnp.exp(-damping * scaled) * weight, 0.0)
     loads[3].wait()
     loads[4].wait()
-    wint[...] = win[...].astype(F32).T.astype(BF16)
-
-    def relay(src, dst):
-        mid[...] = src[...].reshape(1024, 128).astype(F32)
+    wint[...] = (win[...].astype(F32) * 0.5).T.astype(BF16)
+
+    def relay(src, dst, mid):
+        mid[...] = src[...].reshape(512, 128).astype(F32)
         for k in range(N):
-            for j in range(4):
-                dst[k, 16 * j : 16 * j + 16, :] = mid[pl.ds(16 * j + k, N, stride=64), :].astype(BF16)
+            for j in range(2):
+                dst[k, 16 * j : 16 * j + 16, :] = mid[pl.ds(16 * j + k, N, stride=32), :].astype(BF16)
 
     f1_wait()
-    relay(f1_recv, f2_send)
-    f2_start, f2_wait, f2_sent = exchange("grp", f2_send, f2_recv, f2_ss, f2_rs)
+    relay(f1_recv, f2_send, mid)
     f2_start()
     f2_recv[g] = f2_send[g]
+    h1_wait()
+    relay(h1_recv, h2_send, mid2)
+    h2_start()
+    h2_recv[b] = h2_send[b]
 
     tendencies = ("grp", t_send, t_recv, t_ss, t_rs)
+
+    def column_tile(i):
+        x = xb[:, 256 * i : 256 * i + 256]
+        half = lax.dot_general(wint[...], x, nn, preferred_element_type=F32)
+        hidden = (half + half * jnp.tanh(half)).astype(BF16)
+        tend = lax.dot_general(woutt[...], hidden, nn, preferred_element_type=F32)
+        phys[pl.ds(2 * i, 80, stride=16), :] = tend[:, :128]
+        phys[pl.ds(2 * i + 1, 80, stride=16), :] = tend[:, 128:]
 
     @pl.when(g < TILES)
     def _():
@@ -184,18 +208,8 @@
         phys[...] = s_recv[...].reshape(1280, 128).astype(F32)
         for i in range(16):
             xb[:, 128 * i : 128 * i + 128] = phys[pl.ds(i, 80, stride=16), :].astype(BF16)
-        for i in range(8):
-            x = xb[:, 256 * i : 256 * i + 256]
-            half = lax.dot_general(wint[...], x, nn, preferred_element_type=F32) * 0.5
-            hidden = (half + half * jnp.tanh(half)).astype(BF16)
-            tend = lax.dot_general(woutt[...], hidden, nn, preferred_element_type=F32)
-            phys[pl.ds(2 * i, 80, stride=16), :] = tend[:, :128]
-            phys[pl.ds(2 * i + 1, 80, stride=16), :] = tend[:, 128:]
-        t_send[...] = phys[...].reshape(N, 80, 128).astype(BF16)
-
-        for other in targets("grp"):
-            message(*tendencies, other).start()
-        t_recv[g] = t_send[g]
+        for i in range(EARLY):
+            column_tile(i)
 
     f1_sent()
 
@@ -207,11 +221,13 @@
     def _():
         bulk(*states, TILES).wait_send()
 
+    h1_sent()
     f2_wait()
-    mid[...] = f2_recv[...].reshape(1024, 128).astype(F32)
+    mid[...] = f2_recv[...].reshape(512, 128).astype(F32)
+    h2_wait()
     left = lax.broadcasted_iota(jnp.int32, (LAT, 128), 1) < 64
     for k in range(N):
-        part = jnp.concatenate([mid[pl.ds(16 * j + k, N, stride=64), :] for j in range(4)], 0)
+        part = jnp.concatenate([mid[pl.ds(16 * j + k, N, stride=32), :] for j in range(2)] + [h2_recv[k].astype(F32)], 0)
         turned = jnp.concatenate([part, part], 0).T
         at = slice(LAT * k, LAT * k + LAT)
         zf[at, 0:128] = jnp.where(left, turned[0:24], turned[24:48])
@@ -226,17 +242,41 @@
         at = slice(LAT * k, LAT * k + LAT)
         t0, t1, t2 = zf[at, 0:128], zf[at, 128:256], zf[at, 256:384]
         turned = jnp.concatenate([t0, t0, t1, t1, t2, jnp.zeros((8, 128), F32)], 0).T
-        b1_send[k] = jnp.where(odd_chan, turned[64:128], turned[0:64]).astype(BF16)
+        turned = jnp.where(odd_chan, turned[64:128], turned[0:64])
+        b1_send[k] = turned[0:32].astype(BF16)
+        mid2[32 * k : 32 * k + 32, :] = turned[32:64]
+    for k in range(N):
+        for j in range(2):
+            c1_send[k, 16 * j : 16 * j + 16, :] = mid2[pl.ds(16 * j + k, N, stride=32), :].astype(BF16)
 
     b1_start, b1_wait, b1_sent = exchange("band", b1_send, b1_recv, b1_ss, b1_rs)
+    b2_start, b2_wait, b2_sent = exchange("grp", b2_send, b2_recv, b2_ss, b2_rs)
+    c1_start, c1_wait, c1_sent = exchange("grp", c1_send, c1_recv, c1_ss, c1_rs)
+    c2_start, c2_wait, c2_sent = exchange("band", c2_send, c2_recv, c2_ss, c2_rs)
+    c1_start()
     b1_start()
     b1_recv[b] = b1_send[b]
+    c1_recv[g] = c1_send[g]
+
+    @pl.when(g < TILES)
+    def _():
+        for i in range(EARLY, 8):
+            column_tile(i)
+        t_send[...] = phys[...].reshape(N, 80, 128).astype(BF16)
+        for other in targets("grp"):
+            message(*tendencies, other).start()
+        t_recv[g] = t_send[g]
+
     f2_sent()
+    h2_sent()
     b1_wait()
-    relay(b1_recv, b2_send)
-    b2_start, b2_wait, b2_sent = exchange("grp", b2_send, b2_recv, b2_ss, b2_rs)
+    relay(b1_recv, b2_send, mid)
     b2_start()
     b2_recv[g] = b2_send[g]
+    c1_wait()
+    relay(c1_recv, c2_send, mid2)
+    c2_start()
+    c2_recv[b] = c2_send[b]
 
     @pl.when(g < TILES)
     def _():
@@ -254,11 +294,15 @@
             out_ref[:, 8 * a : 8 * a + 8, 256 * lp + 128 : 256 * lp + 256] = block[:, 8:16]
 
     b1_sent()
+    c1_sent()
     b2_wait()
+    c2_wait()
     natural = []
     for j in range(4):
-        slots = b2_recv[:, 16 * j : 16 * j + 16, :].reshape(256, 128).astype(F32).T.astype(BF16)
-        natural.append(lax.dot_general(slots, oh[...], nn, preferred_element_type=F32).astype(BF16))
+        src, order = (b2_recv, oh) if j < 2 else (c2_recv, ohbg)
+        at = 16 * (j % 2)
+        slots = src[:, at : at + 16, :].reshape(256, 128).astype(F32).T.astype(BF16)
+        natural.append(lax.dot_general(slots, order[...], nn, preferred_element_type=F32).astype(BF16))
     n0, n1, n2, n3 = natural
     even = jnp.concatenate([n0[:, :128], n1[:, :128], n2[:, 128:], n3[:, 128:]], 1)
     odd = jnp.concatenate([n0[:, 128:], n1[:, 128:], n2[:, :128], n3[:, :128]], 1)
@@ -270,20 +314,21 @@
     out_ref[:, :, HALF:] += east
 
     b2_sent()
+    c2_sent()
 
 
 def shards(state, pair_of_slot, legendre, diffusion, w_in, w_out):
+    far = lambda x: pltpu.with_memory_space_constraint(x, pltpu.HBM)
     table = jnp.asarray(transform_table())
     hbm = pl.BlockSpec(memory_space=pltpu.HBM)
-    smem = pl.BlockSpec(memory_space=pltpu.SMEM)
     vmem = pl.BlockSpec(memory_space=pltpu.VMEM)
     dma = pltpu.SemaphoreType.DMA
-    message = pltpu.VMEM((N, 64, 128), BF16)
+    message = pltpu.VMEM((N, 32, 128), BF16)
     block = pltpu.VMEM((N, 80, 128), BF16)
     return pl.pallas_call(
         kernel,
-        out_shape=jax.ShapeDtypeStruct(state.shape, F32),
-        in_specs=[hbm, smem, vmem, hbm, smem, hbm, hbm, hbm],
+        out_shape=pltpu.VMEM(state.shape, F32),
+        in_specs=[hbm] * 8,
         out_specs=vmem,
         scratch_shapes=[
             pltpu.VMEM(state.shape, F32),
@@ -291,9 +336,12 @@
             pltpu.VMEM((513, 1, 384), F32),
             pltpu.VMEM((80, 1024), BF16),
             pltpu.VMEM((80, 1024), BF16),
+            pltpu.SMEM((256,), jnp.int32),
+            pltpu.VMEM((1, 256), jnp.int32),
+            pltpu.SMEM((80,), F32),
             *[block] * 4,
-            *[message] * 8,
-            pltpu.VMEM((1024, 128), F32),
+            *[message] * 16,
+            *[pltpu.VMEM((512, 128), F32)] * 2,
             pltpu.VMEM((1280, 128), F32),
             pltpu.VMEM((80, 2048), BF16),
             pltpu.VMEM((384, 384), F32),
@@ -304,14 +352,17 @@
             pltpu.VMEM((512, 128), F32),
             pltpu.VMEM((256, 256), BF16),
             pltpu.VMEM((256, 256), BF16),
-            dma((5,)),
-            *[dma] * 12,
+            dma((8,)),
+            *[dma] * 20,
         ],
         compiler_params=pltpu.CompilerParams(
-            collective_id=0, has_side_effects=True, vmem_limit_bytes=56 * 1024 * 1024
+            collective_id=0, has_side_effects=True, vmem_limit_bytes=40 * 1024 * 1024
         ),
         cost_estimate=pl.CostEstimate(flops=2_500_000_000, bytes_accessed=4_000_000, transcendentals=2_400_000),
-    )(state, pair_of_slot, pair_of_slot.reshape(1, 256), jnp.swapaxes(legendre, 0, 1), diffusion, w_in, w_out.T, table)
+    )(
+        far(state), far(pair_of_slot), far(pair_of_slot.reshape(1, 256)), far(jnp.swapaxes(legendre, 0, 1)),
+        far(diffusion), far(w_in), far(w_out.T), far(table)
+    )
 
 
 def solution(mesh):

time: 47 us -> 43.7 us (0.930)
  Pallas kernels: 44.9 us -> 42.8 us
  local copies, waits for them, and re-layouts: 1.94 us -> 0.83 us
    pallas_call x1, Pallas kernels: 44.9 us -> 42.8 us  [shards(): pl.pallas_call(kernel, out_shape=pltpu.VMEM(state.shape, F32), in_specs=[...]
    unnamed x1, local copies, waits for them, and re-layouts: 1.94 us -> 0.83 us
where the time goes in v2:
time: 43.7 us; the launch traced here: 43.6 us
  Pallas kernels  42.8 us (98%)
  local copies, waits for them, and re-layouts  0.83 us (2%)
    pallas_call x1, Pallas kernels, shards(): pl.pallas_call(kernel, out_shape=pltpu.VMEM(state.shape, F32), in_specs=[...  42.8 us

profile of v2, /device:TPU:1, one launch (start us, length us, event | category | flops | bytes accessed | tf_op | source)
XLA Modules:
  0.0 43.6 jit_solution(13321587831592176850)
XLA Ops:
  0.0 42.8 %shard_map.73 = f32[5,24,1280]{2,1,0:T(8,128)S(1)} custom-call(f32[5,24,1280]{2,1,0:T(8,128)} %state_h.1, s32[256]{0:T(256)} %pair_h.1, s32[1,256]{1,0:T(1,128)} %bitcast.5, f32[513,1,384]{2,1,0:T(1,128)} %bitcast.3, f32[80]{0:T(128)} %diff_h.1, bf16[80,1024]{1,0:T(8,128)(2,1)} %win_h.1, bf16[80,1024]{1,0:T(8,128)(2,1)} %bitcast.4, ...), custom_call_target="tpu_custom_call" | custom-call | flops 2500000000 | bytes 4000000 | tf_op jit(solution)/shard_map/pallas_call | solution.py:328
  42.8 0.8 %copy.9 = f32[5,24,1280]{2,1,0:T(8,128)} copy(f32[5,24,1280]{2,1,0:T(8,128)S(1)} %shard_map.73) | data formatting | bytes 1228800

commit v3 on v2

--- a/solution.py
+++ b/solution.py
@@ -15,7 +15,6 @@
 LAT = 24
 N = 16
 ROWS = 528
-EARLY = 4
 TILES = 15
 F32 = jnp.float32
 BF16 = jnp.bfloat16
@@ -41,8 +40,8 @@
     s_send, s_recv, t_send, t_recv,
     f1_send, f1_recv, f2_send, f2_recv, h1_send, h1_recv, h2_send, h2_recv,
     b1_send, b1_recv, b2_send, b2_recv, c1_send, c1_recv, c2_send, c2_recv,
-    mid, mid2, phys, xb, zf, fac, legb, legt, wint, ohf, oh, ohbg,
-    load_sem, s_ss, s_rs, t_ss, t_rs,
+    mid, mid2, phys, phys2, xb, zf, fac, legb, legt, wint, ohf, oh, ohbg,
+    load_sem, s_ss, s_rs, t_ss, t_rs, s2_ss, s2_rs, t2_ss, t2_rs,
     f1_ss, f1_rs, f2_ss, f2_rs, h1_ss, h1_rs, h2_ss, h2_rs,
     b1_ss, b1_rs, b2_ss, b2_rs, c1_ss, c1_rs, c2_ss, c2_rs,
 ):
@@ -80,19 +79,21 @@
             lax.rem(b // 4 + y, 4) * 4 + lax.rem(b // 2 % 2 + x, 2) * 2 + lax.rem(b % 2 + c, 2) for y, x, c in steps[:-1]
         ]
 
-    def message(axis, src, dst, ss, rs, other):
+    def message(axis, src, dst, ss, rs, rows, other):
         return pltpu.make_async_remote_copy(
-            src_ref=src.at[other], dst_ref=dst.at[{"grp": g, "band": b}[axis]], send_sem=ss, recv_sem=rs,
+            src_ref=src.at[other, rows], dst_ref=dst.at[{"grp": g, "band": b}[axis], rows], send_sem=ss, recv_sem=rs,
             device_id={axis: other}, device_id_type=pl.DeviceIdType.MESH,
         )
 
-    def bulk(axis, src, dst, ss, rs, count):
+    def bulk(axis, src, dst, ss, rs, rows, count):
         return pltpu.make_async_remote_copy(
-            src_ref=src.at[pl.ds(0, count)], dst_ref=dst.at[pl.ds(0, count)], send_sem=ss, recv_sem=rs,
+            src_ref=src.at[pl.ds(0, count), rows], dst_ref=dst.at[pl.ds(0, count), rows], send_sem=ss, recv_sem=rs,
             device_id={axis: lax.rem({"grp": g, "band": b}[axis] + 1, N)}, device_id_type=pl.DeviceIdType.MESH,
         )
 
     def exchange(*refs):
+        refs = (*refs, pl.ds(0, 32))
+
         def start():
             for other in targets(refs[0]):
                 message(*refs, other).start()
@@ -103,7 +104,7 @@
     for a in range(3):
         for lp in range(5):
             block = st[:, 8 * a : 8 * a + 8, 256 * lp : 256 * lp + 256]
-            stacked = jnp.concatenate([block[:, :, :128], block[:, :, 128:]], axis=1)
+            stacked = jnp.concatenate([block[:, :, :128], block[:, :, 128:]], axis=0)
             s_send[a * 5 + lp] = stacked.reshape(80, 128).astype(BF16)
 
     rows = st[...].reshape(C5 * LAT, NLON)
@@ -139,13 +140,17 @@
     pl.semaphore_wait(barrier, 2 * (N - 1))
     h1_start()
     f1_start()
-    states = ("grp", s_send, s_recv, s_ss, s_rs)
-    for other in targets("grp"):
-
-        @pl.when(other < TILES)
-        def _(other=other):
-            message(*states, other).start()
-
+    states = ("grp", s_send, s_recv, s_ss, s_rs, pl.ds(0, 48))
+    states2 = ("grp", s_send, s_recv, s2_ss, s2_rs, pl.ds(48, 32))
+
+    def send_states(part):
+        for other in targets("grp"):
+
+            @pl.when(other < TILES)
+            def _(other=other):
+                message(*part, other).start()
+
+    send_states(states)
     f1_recv[b] = f1_send[b]
     h1_recv[g] = h1_send[g]
 
@@ -185,41 +190,48 @@
     f1_wait()
     relay(f1_recv, f2_send, mid)
     f2_start()
+    send_states(states2)
     f2_recv[g] = f2_send[g]
     h1_wait()
     relay(h1_recv, h2_send, mid2)
     h2_start()
     h2_recv[b] = h2_send[b]
 
-    tendencies = ("grp", t_send, t_recv, t_ss, t_rs)
-
-    def column_tile(i):
-        x = xb[:, 256 * i : 256 * i + 256]
-        half = lax.dot_general(wint[...], x, nn, preferred_element_type=F32)
-        hidden = (half + half * jnp.tanh(half)).astype(BF16)
-        tend = lax.dot_general(woutt[...], hidden, nn, preferred_element_type=F32)
-        phys[pl.ds(2 * i, 80, stride=16), :] = tend[:, :128]
-        phys[pl.ds(2 * i + 1, 80, stride=16), :] = tend[:, 128:]
+    tendencies = ("grp", t_send, t_recv, t_ss, t_rs, pl.ds(0, 32))
+    tendencies2 = ("grp", t_send, t_recv, t2_ss, t2_rs, pl.ds(32, 48))
+
+    def column_half(buffer):
+        for i in range(8):
+            xb[:, 128 * i : 128 * i + 128] = buffer[pl.ds(i, 80, stride=8), :].astype(BF16)
+        for i in range(4):
+            x = xb[:, 256 * i : 256 * i + 256]
+            half = lax.dot_general(wint[...], x, nn, preferred_element_type=F32)
+            hidden = (half + half * jnp.tanh(half)).astype(BF16)
+            tend = lax.dot_general(woutt[...], hidden, nn, preferred_element_type=F32)
+            buffer[pl.ds(2 * i, 80, stride=8), :] = tend[:, :128]
+            buffer[pl.ds(2 * i + 1, 80, stride=8), :] = tend[:, 128:]
 
     @pl.when(g < TILES)
     def _():
         s_recv[g] = s_send[g]
         bulk(*states, N - 1).wait_recv()
-        phys[...] = s_recv[...].reshape(1280, 128).astype(F32)
-        for i in range(16):
-            xb[:, 128 * i : 128 * i + 128] = phys[pl.ds(i, 80, stride=16), :].astype(BF16)
-        for i in range(EARLY):
-            column_tile(i)
+        phys[...] = s_recv[:, 0:48, :].astype(F32)[:, 0:40].reshape(640, 128)
+        column_half(phys)
+        t_send[:, 0:32, :] = phys[...].reshape(N, 40, 128)[:, 0:32].astype(BF16)
+        for other in targets("grp"):
+            message(*tendencies, other).start()
 
     f1_sent()
 
     @pl.when(g < TILES)
     def _():
         bulk(*states, TILES - 1).wait_send()
+        bulk(*states2, TILES - 1).wait_send()
 
     @pl.when(g >= TILES)
     def _():
         bulk(*states, TILES).wait_send()
+        bulk(*states2, TILES).wait_send()
 
     h1_sent()
     f2_wait()
@@ -260,11 +272,13 @@
 
     @pl.when(g < TILES)
     def _():
-        for i in range(EARLY, 8):
-            column_tile(i)
-        t_send[...] = phys[...].reshape(N, 80, 128).astype(BF16)
+        bulk(*states2, N - 1).wait_recv()
+        phys2[...] = s_recv[:, 32:80, :].astype(F32)[:, 8:48].reshape(640, 128)
+        column_half(phys2)
+        rest = jnp.concatenate([phys[...].reshape(N, 40, 128)[:, 32:40], phys2[...].reshape(N, 40, 128)], axis=1)
+        t_send[:, 32:80, :] = rest.astype(BF16)
         for other in targets("grp"):
-            message(*tendencies, other).start()
+            message(*tendencies2, other).start()
         t_recv[g] = t_send[g]
 
     f2_sent()
@@ -281,17 +295,20 @@
     @pl.when(g < TILES)
     def _():
         bulk(*tendencies, TILES - 1).wait_recv()
+        bulk(*tendencies2, TILES - 1).wait_recv()
         bulk(*tendencies, N - 1).wait_send()
+        bulk(*tendencies2, N - 1).wait_send()
 
     @pl.when(g >= TILES)
     def _():
         bulk(*tendencies, TILES).wait_recv()
+        bulk(*tendencies2, TILES).wait_recv()
 
     for a in range(3):
         for lp in range(5):
-            block = t_recv[a * 5 + lp].astype(F32).reshape(C5, 16, 128)
-            out_ref[:, 8 * a : 8 * a + 8, 256 * lp : 256 * lp + 128] = block[:, 0:8]
-            out_ref[:, 8 * a : 8 * a + 8, 256 * lp + 128 : 256 * lp + 256] = block[:, 8:16]
+            block = t_recv[a * 5 + lp].astype(F32)
+            out_ref[:, 8 * a : 8 * a + 8, 256 * lp : 256 * lp + 128] = block[0:40].reshape(C5, 8, 128)
+            out_ref[:, 8 * a : 8 * a + 8, 256 * lp + 128 : 256 * lp + 256] = block[40:80].reshape(C5, 8, 128)
 
     b1_sent()
     c1_sent()
@@ -342,8 +359,8 @@
             *[block] * 4,
             *[message] * 16,
             *[pltpu.VMEM((512, 128), F32)] * 2,
-            pltpu.VMEM((1280, 128), F32),
-            pltpu.VMEM((80, 2048), BF16),
+            *[pltpu.VMEM((640, 128), F32)] * 2,
+            pltpu.VMEM((80, 1024), BF16),
             pltpu.VMEM((384, 384), F32),
             pltpu.VMEM((ROWS, 384), F32),
             pltpu.VMEM((ROWS, 384), BF16),
@@ -353,7 +370,7 @@
             pltpu.VMEM((256, 256), BF16),
             pltpu.VMEM((256, 256), BF16),
             dma((8,)),
-            *[dma] * 20,
+            *[dma] * 24,
         ],
         compiler_params=pltpu.CompilerParams(
             collective_id=0, has_side_effects=True, vmem_limit_bytes=40 * 1024 * 1024

time: 43.7 us -> 39.7 us (0.908)
  Pallas kernels: 42.8 us -> 38.7 us
    pallas_call x1, Pallas kernels: 42.8 us -> 38.7 us  [shards(): pl.pallas_call(kernel, out_shape=pltpu.VMEM(state.shape, F32), in_specs=[...]
where the time goes in v3:
time: 39.7 us; the launch traced here: 39.6 us
  Pallas kernels  38.7 us (97%)
  local copies, waits for them, and re-layouts  0.83 us (2%)
    pallas_call x1, Pallas kernels, shards(): pl.pallas_call(kernel, out_shape=pltpu.VMEM(state.shape, F32), in_specs=[...  38.7 us
    unnamed x1, local copies, waits for them, and re-layouts  0.83 us

profile of v3, /device:TPU:1, one launch (start us, length us, event | category | flops | bytes accessed | tf_op | source)
XLA Modules:
  0.0 39.6 jit_solution(2128316167366115507)
XLA Ops:
  0.0 38.7 %shard_map.73 = f32[5,24,1280]{2,1,0:T(8,128)S(1)} custom-call(f32[5,24,1280]{2,1,0:T(8,128)} %state_h.1, s32[256]{0:T(256)} %pair_h.1, s32[1,256]{1,0:T(1,128)} %bitcast.5, f32[513,1,384]{2,1,0:T(1,128)} %bitcast.3, f32[80]{0:T(128)} %diff_h.1, bf16[80,1024]{1,0:T(8,128)(2,1)} %win_h.1, bf16[80,1024]{1,0:T(8,128)(2,1)} %bitcast.4, ...), custom_call_target="tpu_custom_call" | custom-call | flops 2500000000 | bytes 4000000 | tf_op jit(solution)/shard_map/pallas_call | solution.py:345
  38.8 0.8 %copy.9 = f32[5,24,1280]{2,1,0:T(8,128)} copy(f32[5,24,1280]{2,1,0:T(8,128)S(1)} %shard_map.73) | data formatting | bytes 1228800

commit v4 on v3

--- a/solution.py
+++ b/solution.py
@@ -48,25 +48,6 @@
     g = lax.axis_index("grp")
     b = lax.axis_index("band")
 
-    loads = [
-        pltpu.make_async_copy(src, dst, load_sem.at[i])
-        for i, (src, dst) in enumerate(
-            [(state_h, st), (tab_h, tab), (leg_h, leg), (win_h, win), (woutt_h, woutt),
-             (pair_h, pair_s), (pairv_h, pair_v), (diff_h, diff_s)]
-        )
-    ]
-    for load in loads:
-        load.start()
-
-    barrier = pltpu.get_barrier_semaphore()
-
-    def greet(k, carry):
-        pl.semaphore_signal(barrier, inc=1, device_id={"grp": lax.rem(g + k, N)}, device_id_type=pl.DeviceIdType.MESH)
-        pl.semaphore_signal(barrier, inc=1, device_id={"band": lax.rem(b + k, N)}, device_id_type=pl.DeviceIdType.MESH)
-        return carry
-
-    lax.fori_loop(1, N, greet, 0)
-
     def targets(axis):
         if axis == "grp":
             steps = sorted(((x, z) for x in range(2) for z in range(8)), key=lambda s: -(2 * s[0] + min(s[1], 8 - s[1])))
@@ -78,6 +59,21 @@
         return [
             lax.rem(b // 4 + y, 4) * 4 + lax.rem(b // 2 % 2 + x, 2) * 2 + lax.rem(b % 2 + c, 2) for y, x, c in steps[:-1]
         ]
+
+    barrier = pltpu.get_barrier_semaphore()
+    for axis in ("grp", "band"):
+        for other in targets(axis):
+            pl.semaphore_signal(barrier, inc=1, device_id={axis: other}, device_id_type=pl.DeviceIdType.MESH)
+
+    loads = [
+        pltpu.make_async_copy(src, dst, load_sem.at[i])
+        for i, (src, dst) in enumerate(
+            [(state_h, st), (tab_h, tab), (leg_h, leg), (win_h, win), (woutt_h, woutt),
+             (pair_h, pair_s), (pairv_h, pair_v), (diff_h, diff_s)]
+        )
+    ]
+    for load in loads:
+        load.start()
 
     def message(axis, src, dst, ss, rs, rows, other):
         return pltpu.make_async_remote_copy(
@@ -203,13 +199,11 @@
     def column_half(buffer):
         for i in range(8):
             xb[:, 128 * i : 128 * i + 128] = buffer[pl.ds(i, 80, stride=8), :].astype(BF16)
-        for i in range(4):
-            x = xb[:, 256 * i : 256 * i + 256]
-            half = lax.dot_general(wint[...], x, nn, preferred_element_type=F32)
-            hidden = (half + half * jnp.tanh(half)).astype(BF16)
-            tend = lax.dot_general(woutt[...], hidden, nn, preferred_element_type=F32)
-            buffer[pl.ds(2 * i, 80, stride=8), :] = tend[:, :128]
-            buffer[pl.ds(2 * i + 1, 80, stride=8), :] = tend[:, 128:]
+        half = lax.dot_general(wint[...], xb[...], nn, preferred_element_type=F32)
+        hidden = (half + half * jnp.tanh(half)).astype(BF16)
+        tend = lax.dot_general(woutt[...], hidden, nn, preferred_element_type=F32)
+        for i in range(8):
+            buffer[pl.ds(i, 80, stride=8), :] = tend[:, 128 * i : 128 * i + 128]
 
     @pl.when(g < TILES)
     def _():
@@ -218,7 +212,7 @@
         phys[...] = s_recv[:, 0:48, :].astype(F32)[:, 0:40].reshape(640, 128)
         column_half(phys)
         t_send[:, 0:32, :] = phys[...].reshape(N, 40, 128)[:, 0:32].astype(BF16)
-        for other in targets("grp"):
+        for other in reversed(targets("grp")):
             message(*tendencies, other).start()
 
     f1_sent()
@@ -277,7 +271,7 @@
         column_half(phys2)
         rest = jnp.concatenate([phys[...].reshape(N, 40, 128)[:, 32:40], phys2[...].reshape(N, 40, 128)], axis=1)
         t_send[:, 32:80, :] = rest.astype(BF16)
-        for other in targets("grp"):
+        for other in reversed(targets("grp")):
             message(*tendencies2, other).start()
         t_recv[g] = t_send[g]
 

time: 39.7 us -> 39.3 us (0.990)
  Pallas kernels: 38.7 us -> 38.3 us
    pallas_call x1, Pallas kernels: 38.7 us -> 38.3 us  [shards(): pl.pallas_call(kernel, out_shape=pltpu.VMEM(state.shape, F32), in_specs=[...]
where the time goes in v4:
time: 39.3 us; the launch traced here: 39.2 us
  Pallas kernels  38.3 us (97%)
  local copies, waits for them, and re-layouts  0.83 us (2%)
    pallas_call x1, Pallas kernels, shards(): pl.pallas_call(kernel, out_shape=pltpu.VMEM(state.shape, F32), in_specs=[...  38.3 us
    unnamed x1, local copies, waits for them, and re-layouts  0.83 us

profile of v4, /device:TPU:1, one launch (start us, length us, event | category | flops | bytes accessed | tf_op | source)
XLA Modules:
  0.0 39.2 jit_solution(13766365556675223275)
XLA Ops:
  0.0 38.3 %shard_map.73 = f32[5,24,1280]{2,1,0:T(8,128)S(1)} custom-call(f32[5,24,1280]{2,1,0:T(8,128)} %state_h.1, s32[256]{0:T(256)} %pair_h.1, s32[1,256]{1,0:T(1,128)} %bitcast.5, f32[513,1,384]{2,1,0:T(1,128)} %bitcast.3, f32[80]{0:T(128)} %diff_h.1, bf16[80,1024]{1,0:T(8,128)(2,1)} %win_h.1, bf16[80,1024]{1,0:T(8,128)(2,1)} %bitcast.4, ...), custom_call_target="tpu_custom_call" | custom-call | flops 2500000000 | bytes 4000000 | tf_op jit(solution)/shard_map/pallas_call | solution.py:339
  38.3 0.8 %copy.9 = f32[5,24,1280]{2,1,0:T(8,128)} copy(f32[5,24,1280]{2,1,0:T(8,128)S(1)} %shard_map.73) | data formatting | bytes 1228800

commit v5 on v4

--- a/solution.py
+++ b/solution.py
@@ -106,8 +106,13 @@
     rows = st[...].reshape(C5 * LAT, NLON)
     west, east = rows[:, :HALF], rows[:, HALF:]
     pad = jnp.zeros((8, HALF), F32)
-    even = jnp.concatenate([west + east, pad], 0).astype(BF16)
-    odd = jnp.concatenate([west - east, pad], 0).astype(BF16)
+
+    def terms(value):
+        value = jnp.concatenate([value, pad], 0)
+        high = value.astype(BF16)
+        return jnp.concatenate([high, (value - high.astype(F32)).astype(BF16)], 0)
+
+    even, odd = terms(west + east), terms(west - east)
     value = 2 * (lax.broadcasted_iota(jnp.int32, (256, 256), 0) % 128) + lax.broadcasted_iota(jnp.int32, (256, 256), 0) // 128
     loads[6].wait()
     hot = (value == pair_v[...]).astype(F32)
@@ -120,8 +125,10 @@
     loads[1].wait()
     nt = (((1,), (1,)), ((), ()))
     nn = (((1,), (0,)), ((), ()))
-    ce = lax.dot_general(tab[:512, :], even, nt, preferred_element_type=F32).astype(BF16)
-    co = lax.dot_general(tab[512:, :], odd, nt, preferred_element_type=F32).astype(BF16)
+    ce = lax.dot_general(tab[:512, :], even, nt, preferred_element_type=F32)
+    co = lax.dot_general(tab[512:, :], odd, nt, preferred_element_type=F32)
+    ce = (ce[:, :128] + ce[:, 128:]).astype(BF16)
+    co = (co[:, :128] + co[:, 128:]).astype(BF16)
     for j in range(4):
         e, o = ce[128 * j : 128 * j + 128], co[128 * j : 128 * j + 128]
         natural = jnp.concatenate([e, o] if j < 2 else [o, e], 0)
@@ -149,6 +156,22 @@
     send_states(states)
     f1_recv[b] = f1_send[b]
     h1_recv[g] = h1_send[g]
+
+    def relay(src, dst, mid):
+        mid[...] = src[...].reshape(512, 128).astype(F32)
+        for k in range(N):
+            for j in range(2):
+                dst[k, 16 * j : 16 * j + 16, :] = mid[pl.ds(16 * j + k, N, stride=32), :].astype(BF16)
+
+    f1_wait()
+    relay(f1_recv, f2_send, mid)
+    f2_start()
+    send_states(states2)
+    f2_recv[g] = f2_send[g]
+    h1_wait()
+    relay(h1_recv, h2_send, mid2)
+    h2_start()
+    h2_recv[b] = h2_send[b]
 
     loads[5].wait()
     loads[7].wait()
@@ -176,22 +199,6 @@
     loads[3].wait()
     loads[4].wait()
     wint[...] = (win[...].astype(F32) * 0.5).T.astype(BF16)
-
-    def relay(src, dst, mid):
-        mid[...] = src[...].reshape(512, 128).astype(F32)
-        for k in range(N):
-            for j in range(2):
-                dst[k, 16 * j : 16 * j + 16, :] = mid[pl.ds(16 * j + k, N, stride=32), :].astype(BF16)
-
-    f1_wait()
-    relay(f1_recv, f2_send, mid)
-    f2_start()
-    send_states(states2)
-    f2_recv[g] = f2_send[g]
-    h1_wait()
-    relay(h1_recv, h2_send, mid2)
-    h2_start()
-    h2_recv[b] = h2_send[b]
 
     tendencies = ("grp", t_send, t_recv, t_ss, t_rs, pl.ds(0, 32))
     tendencies2 = ("grp", t_send, t_recv, t2_ss, t2_rs, pl.ds(32, 48))

time: 39.3 us -> 39.5 us (level)
  no operation moved by 1% of the time
where the time goes in v5:
time: 39.5 us; the launch traced here: 39.4 us
  Pallas kernels  38.6 us (98%)
  local copies, waits for them, and re-layouts  0.83 us (2%)
    pallas_call x1, Pallas kernels, shards(): pl.pallas_call(kernel, out_shape=pltpu.VMEM(state.shape, F32), in_specs=[...  38.6 us
    unnamed x1, local copies, waits for them, and re-layouts  0.83 us

profile of v5, /device:TPU:1, one launch (start us, length us, event | category | flops | bytes accessed | tf_op | source)
XLA Modules:
  0.0 39.4 jit_solution(16901246426551192910)
XLA Ops:
  0.0 38.6 %shard_map.73 = f32[5,24,1280]{2,1,0:T(8,128)S(1)} custom-call(f32[5,24,1280]{2,1,0:T(8,128)} %state_h.1, s32[256]{0:T(256)} %pair_h.1, s32[1,256]{1,0:T(1,128)} %bitcast.5, f32[513,1,384]{2,1,0:T(1,128)} %bitcast.3, f32[80]{0:T(128)} %diff_h.1, bf16[80,1024]{1,0:T(8,128)(2,1)} %win_h.1, bf16[80,1024]{1,0:T(8,128)(2,1)} %bitcast.4, ...), custom_call_target="tpu_custom_call" | custom-call | flops 2500000000 | bytes 4000000 | tf_op jit(solution)/shard_map/pallas_call | solution.py:346
  38.6 0.8 %copy.9 = f32[5,24,1280]{2,1,0:T(8,128)} copy(f32[5,24,1280]{2,1,0:T(8,128)S(1)} %shard_map.73) | data formatting | bytes 1228800

commit v6 on v5

--- a/solution.py
+++ b/solution.py
@@ -72,8 +72,8 @@
              (pair_h, pair_s), (pairv_h, pair_v), (diff_h, diff_s)]
         )
     ]
-    for load in loads:
-        load.start()
+    for i in (6, 0, 1):
+        loads[i].start()
 
     def message(axis, src, dst, ss, rs, rows, other):
         return pltpu.make_async_remote_copy(
@@ -96,23 +96,6 @@
 
         return start, bulk(*refs, N - 1).wait_recv, bulk(*refs, N - 1).wait_send
 
-    loads[0].wait()
-    for a in range(3):
-        for lp in range(5):
-            block = st[:, 8 * a : 8 * a + 8, 256 * lp : 256 * lp + 256]
-            stacked = jnp.concatenate([block[:, :, :128], block[:, :, 128:]], axis=0)
-            s_send[a * 5 + lp] = stacked.reshape(80, 128).astype(BF16)
-
-    rows = st[...].reshape(C5 * LAT, NLON)
-    west, east = rows[:, :HALF], rows[:, HALF:]
-    pad = jnp.zeros((8, HALF), F32)
-
-    def terms(value):
-        value = jnp.concatenate([value, pad], 0)
-        high = value.astype(BF16)
-        return jnp.concatenate([high, (value - high.astype(F32)).astype(BF16)], 0)
-
-    even, odd = terms(west + east), terms(west - east)
     value = 2 * (lax.broadcasted_iota(jnp.int32, (256, 256), 0) % 128) + lax.broadcasted_iota(jnp.int32, (256, 256), 0) // 128
     loads[6].wait()
     hot = (value == pair_v[...]).astype(F32)
@@ -122,6 +105,18 @@
         for k in range(N):
             turned = ohf[pl.ds(256 * h + k, N, stride=N), :].astype(BF16)
             ohbg[k * N : (k + 1) * N, 128 * h : 128 * h + 128] = turned
+
+    loads[0].wait()
+    rows = st[...].reshape(C5 * LAT, NLON)
+    west, east = rows[:, :HALF], rows[:, HALF:]
+    pad = jnp.zeros((8, HALF), F32)
+
+    def terms(value):
+        value = jnp.concatenate([value, pad], 0)
+        high = value.astype(BF16)
+        return jnp.concatenate([high, (value - high.astype(F32)).astype(BF16)], 0)
+
+    even, odd = terms(west + east), terms(west - east)
     loads[1].wait()
     nt = (((1,), (1,)), ((), ()))
     nn = (((1,), (0,)), ((), ()))
@@ -143,6 +138,15 @@
     pl.semaphore_wait(barrier, 2 * (N - 1))
     h1_start()
     f1_start()
+    for i in (2, 3, 4, 5, 7):
+        loads[i].start()
+
+    for a in range(3):
+        for lp in range(5):
+            block = st[:, 8 * a : 8 * a + 8, 256 * lp : 256 * lp + 256]
+            stacked = jnp.concatenate([block[:, :, :128], block[:, :, 128:]], axis=0)
+            s_send[a * 5 + lp] = stacked.reshape(80, 128).astype(BF16)
+
     states = ("grp", s_send, s_recv, s_ss, s_rs, pl.ds(0, 48))
     states2 = ("grp", s_send, s_recv, s2_ss, s2_rs, pl.ds(48, 32))
 

time: 39.5 us -> 39.1 us (0.990)
  Pallas kernels: 38.6 us -> 38.2 us
where the time goes in v6:
time: 39.1 us; the launch traced here: 39 us
  Pallas kernels  38.2 us (98%)
  local copies, waits for them, and re-layouts  0.83 us (2%)
    pallas_call x1, Pallas kernels, shards(): pl.pallas_call(kernel, out_shape=pltpu.VMEM(state.shape, F32), in_specs=[...  38.2 us
    unnamed x1, local copies, waits for them, and re-layouts  0.83 us

profile of v6, /device:TPU:1, one launch (start us, length us, event | category | flops | bytes accessed | tf_op | source)
XLA Modules:
  0.0 39.0 jit_solution(15503337917014113430)
XLA Ops:
  0.0 38.2 %shard_map.73 = f32[5,24,1280]{2,1,0:T(8,128)S(1)} custom-call(f32[5,24,1280]{2,1,0:T(8,128)} %state_h.1, s32[256]{0:T(256)} %pair_h.1, s32[1,256]{1,0:T(1,128)} %bitcast.5, f32[513,1,384]{2,1,0:T(1,128)} %bitcast.3, f32[80]{0:T(128)} %diff_h.1, bf16[80,1024]{1,0:T(8,128)(2,1)} %win_h.1, bf16[80,1024]{1,0:T(8,128)(2,1)} %bitcast.4, ...), custom_call_target="tpu_custom_call" | custom-call | flops 2500000000 | bytes 4000000 | tf_op jit(solution)/shard_map/pallas_call | solution.py:350
  38.2 0.8 %copy.9 = f32[5,24,1280]{2,1,0:T(8,128)} copy(f32[5,24,1280]{2,1,0:T(8,128)S(1)} %shard_map.73) | data formatting | bytes 1228800

commit v7 on v6

--- a/solution.py
+++ b/solution.py
@@ -135,17 +135,17 @@
     f2_start, f2_wait, f2_sent = exchange("grp", f2_send, f2_recv, f2_ss, f2_rs)
     h1_start, h1_wait, h1_sent = exchange("grp", h1_send, h1_recv, h1_ss, h1_rs)
     h2_start, h2_wait, h2_sent = exchange("band", h2_send, h2_recv, h2_ss, h2_rs)
+    for a in range(3):
+        for lp in range(5):
+            block = st[:, 8 * a : 8 * a + 8, 256 * lp : 256 * lp + 256]
+            stacked = jnp.concatenate([block[:, :, :128], block[:, :, 128:]], axis=0)
+            s_send[a * 5 + lp] = stacked.reshape(80, 128).astype(BF16)
+
     pl.semaphore_wait(barrier, 2 * (N - 1))
     h1_start()
     f1_start()
     for i in (2, 3, 4, 5, 7):
         loads[i].start()
-
-    for a in range(3):
-        for lp in range(5):
-            block = st[:, 8 * a : 8 * a + 8, 256 * lp : 256 * lp + 256]
-            stacked = jnp.concatenate([block[:, :, :128], block[:, :, 128:]], axis=0)
-            s_send[a * 5 + lp] = stacked.reshape(80, 128).astype(BF16)
 
     states = ("grp", s_send, s_recv, s_ss, s_rs, pl.ds(0, 48))
     states2 = ("grp", s_send, s_recv, s2_ss, s2_rs, pl.ds(48, 32))

time: 39.1 us -> 39.1 us (level)
  no operation moved by 1% of the time
where the time goes in v7:
time: 39.1 us; the launch traced here: 39 us
  Pallas kernels  38.2 us (98%)
  local copies, waits for them, and re-layouts  0.83 us (2%)
    pallas_call x1, Pallas kernels, shards(): pl.pallas_call(kernel, out_shape=pltpu.VMEM(state.shape, F32), in_specs=[...  38.2 us
    unnamed x1, local copies, waits for them, and re-layouts  0.83 us

profile of v7, /device:TPU:1, one launch (start us, length us, event | category | flops | bytes accessed | tf_op | source)
XLA Modules:
  0.0 39.0 jit_solution(13890299690244626308)
XLA Ops:
  0.0 38.2 %shard_map.73 = f32[5,24,1280]{2,1,0:T(8,128)S(1)} custom-call(f32[5,24,1280]{2,1,0:T(8,128)} %state_h.1, s32[256]{0:T(256)} %pair_h.1, s32[1,256]{1,0:T(1,128)} %bitcast.5, f32[513,1,384]{2,1,0:T(1,128)} %bitcast.3, f32[80]{0:T(128)} %diff_h.1, bf16[80,1024]{1,0:T(8,128)(2,1)} %win_h.1, bf16[80,1024]{1,0:T(8,128)(2,1)} %bitcast.4, ...), custom_call_target="tpu_custom_call" | custom-call | flops 2500000000 | bytes 4000000 | tf_op jit(solution)/shard_map/pallas_call | solution.py:350
  38.2 0.8 %copy.9 = f32[5,24,1280]{2,1,0:T(8,128)} copy(f32[5,24,1280]{2,1,0:T(8,128)S(1)} %shard_map.73) | data formatting | bytes 1228800
